TPU v7x, 512 devices: a whole 4x4x16 slice. The times are simulated.
512 devices in a mesh: row: 16 (over x, y_lo, core), col: 32 (over y_hi, z).
Axes of the slice: x: 4, y: 4 (y_hi: 2, y_lo: 2; y = y_hi * 2 + y_lo), z: 16, core: 2. Of those that a mesh axis runs over, the one named last changes fastest.
Arguments:
- interactions: bfloat16 [4096, 8192], P('col', 'row'), may hold values from -1 to 1
- regular: float32 [4096], P('col'), may hold values from 0.2 to 2
Outputs:
- factored: float32 [4, 1024, 4096], P(None, 'row', 'col')
All inputs are finite; a program needn't handle non-finite values.
Results may differ from a plain program's by a relative error of at most 0.0003.
Values may be sent and summed in bfloat16 or wider, within the bound.
A program may use at most 128 MiB of HBM per device.

v0:
```python
import jax
import jax.numpy as jnp
from jax import lax
from jax.sharding import PartitionSpec as P

PANEL = 1024
SPAN = 4


def from_root(value, axis, source):
    kept = jnp.where(lax.axis_index(axis) == source, value, 0).astype(value.dtype)
    return lax.psum(kept, axis)


def body(interactions, regular):
    row_count = lax.axis_size("row")
    row_index = lax.axis_index("row")
    col_index = lax.axis_index("col")
    block_width = interactions.shape[0]
    user_count = interactions.shape[1]
    band_rows = PANEL // row_count
    per_owner = SPAN * band_rows
    panel_blocks = PANEL // block_width
    highest = lax.Precision.HIGHEST
    everyone = lax.all_gather(interactions, "col", axis=0, tiled=True)
    grouped = everyone.reshape(SPAN, row_count, band_rows, user_count)
    term_block = jnp.einsum(
        "kotu,ju->oktj", grouped, interactions, preferred_element_type=jnp.float32
    )
    grid_tile = lax.psum_scatter(
        term_block.reshape(per_owner * lax.axis_size("row"), block_width),
        "row",
        scatter_dimension=0,
        tiled=True,
    ).reshape(SPAN, band_rows, block_width)
    row_items = (
        jnp.arange(SPAN, dtype=jnp.int32)[:, None] * PANEL
        + row_index * band_rows
        + jnp.arange(band_rows, dtype=jnp.int32)[None, :]
    )
    col_items = col_index * block_width + jnp.arange(block_width, dtype=jnp.int32)
    on_diagonal = row_items[:, :, None] == col_items[None, None, :]
    grid_tile = grid_tile + jnp.where(on_diagonal, regular[None, None, :], jnp.float32(0.0))
    row_band = lax.all_gather(grid_tile, "col", axis=2, tiled=True)
    corner = row_band[0, :, :PANEL]
    diagonal = lax.all_gather(corner, "row", axis=0, tiled=True)
    lower_factor = jnp.linalg.cholesky(diagonal)
    inverse = lax.linalg.triangular_solve(
        lower_factor, jnp.eye(PANEL, dtype=jnp.float32), left_side=True, lower=True
    )
    col_slot = col_index * block_width // PANEL
    first_owner = col_index * block_width % PANEL // band_rows
    lower_rows = row_band[1:, :, :PANEL].reshape((SPAN - 1) * band_rows, PANEL)
    left_own = jnp.dot(lower_rows, inverse.T, precision=highest)
    offered = lax.dynamic_slice_in_dim(
        left_own, jnp.maximum(col_slot - 1, 0) * band_rows, band_rows, 0
    )
    pieces = []
    for half_index in range(block_width // band_rows):
        pieces.append(from_root(offered, "row", first_owner + half_index))
    left_cols = jnp.concatenate(pieces, 0)
    current = grid_tile[1:].reshape((SPAN - 1) * band_rows, block_width)
    trailing = current - jnp.einsum("ia,ja->ij", left_own, left_cols, precision=highest)
    column_slot = jnp.minimum(col_index, panel_blocks - 1)
    lower_tile = lax.dynamic_slice(
        lower_factor, (row_index * band_rows, column_slot * block_width), (band_rows, block_width)
    )
    left_tile = lax.dynamic_slice_in_dim(left_own, column_slot * block_width, block_width, 1)
    in_panel = col_index < panel_blocks
    first_part = jnp.where(in_panel, lower_tile, jnp.zeros_like(lower_tile))
    other_parts = jnp.where(in_panel, left_tile, trailing).reshape(SPAN - 1, band_rows, block_width)
    return jnp.concatenate([first_part[None], other_parts], 0)


def solution(mesh):
    return jax.shard_map(
        body,
        mesh=mesh,
        in_specs=(P("col", "row"), P("col")),
        out_specs=P(None, "row", "col"),
        check_vma=False,
    )
```

profile of v0, /device:TPU:1, one launch (start us, length us, event | category | flops | bytes accessed | tf_op | source)
XLA Modules:
  0.0 960.7 jit_solution(6889385909888078004)
XLA Ops:
  7.3 164.6 %all-gather.5.cloned.1.call-done = bf16[4096,512]{1,0:T(8,128)(2,1)} async-done(((bf16[128,512]{1,0:T(8,128)(2,1)}), bf16[4096,512]{1,0:T(8,128)(2,1)}) %all-gather.5.cloned.1.call-update) | async-done | bytes 4194320 | tf_op jit(solution)/shard_map/all_gather | solution.py:25
  171.9 3.5 convolution_bitcast_fusion
  175.5 1.5 copy.9
  177.1 71.5 %reduce-scatter.2.cloned.1.call-done = f32[256,128]{1,0:T(8,128)} async-done(((f32[4096,128]{1,0:T(8,128)}), f32[256,128]{1,0:T(8,128)}) %reduce-scatter.2.cloned.1.call-update) | async-done | bytes 131088 | tf_op jit(solution)/shard_map/reduce_scatter | solution.py:30
  248.6 1.7 select_add_fusion
  250.4 160.2 %all-gather.7.cloned.1.call-done = f32[4,64,4096]{2,1,0:T(8,128)} async-done(((f32[4,64,128]{2,1,0:T(8,128)}), f32[4,64,4096]{2,1,0:T(8,128)}) %all-gather.7.cloned.1.call-update) | async-done | bytes 4194320 | tf_op jit(solution)/shard_map/all_gather | solution.py:44
  410.5 1.0 slice.246
  411.5 1.0 copy.10
  413.0 2.4 fusion.23
  415.4 1.2 slice.247
  416.6 43.8 %all-gather.9.cloned.1.call-done = f32[1,1024,1024]{2,0,1:T(1,128)} async-done(((f32[1,64,1024]{2,0,1:T(1,128)}), f32[1,1024,1024]{2,0,1:T(1,128)}) %all-gather.9.cloned.1.call-update) | async-done | bytes 4194320 | tf_op jit(solution)/shard_map/all_gather | solution.py:46
  460.4 11.1 %copy.11 = f32[1,1024,1024]{1,2,0:T(8,128)} copy(f32[1,1024,1024]{2,0,1:T(1,128)} %all-gather.9.cloned.1.call-done) | data formatting | bytes 8388608 | tf_op jit(solution)/shard_map/all_gather | solution.py:46
  471.5 5.0 fusion
  476.5 2.0 copy-done.1
  478.5 11.7 %cholesky.223 = f32[128,128]{1,0:T(8,128)S(1)} custom-call(f32[128,128]{1,0:T(8,128)S(1)} %cholesky.580), custom_call_target="Cholesky" | custom-call | tf_op jit(solution)/shard_map/jit(cholesky)/cholesky | solution.py:47
  490.2 9.8 %custom-call.62 = f32[1,128,128]{1,2,0:T(8,128)S(1)} custom-call(f32[1,128,128]{2,1,0:T(8,128)S(1)} %get-tuple-element.75), custom_call_target="InvertDiagBlocksLowerTriangular" | custom-call | tf_op jit(solution)/shard_map/jit(cholesky)/cholesky | solution.py:47
  500.1 2.5 cholesky.255
  502.5 2.4 constant_dynamic-update-slice_fusion.31
  504.9 1.5 convolution_subtract_fusion.5
  506.5 11.9 %cholesky.244 = f32[128,128]{1,0:T(8,128)S(1)} custom-call(f32[128,128]{1,0:T(8,128)S(1)} %cholesky.584), custom_call_target="Cholesky" | custom-call | tf_op jit(solution)/shard_map/jit(cholesky)/cholesky | solution.py:47
  519.0 9.8 %custom-call.63 = f32[1,128,128]{1,2,0:T(8,128)S(1)} custom-call(f32[1,128,128]{2,1,0:T(8,128)S(1)} %get-tuple-element.72), custom_call_target="InvertDiagBlocksLowerTriangular" | custom-call | tf_op jit(solution)/shard_map/jit(cholesky)/cholesky | solution.py:47
  528.9 1.2 convolution_dynamic-update-slice_fusion.1
  530.1 2.1 convolution_subtract_fusion.6
  532.2 11.7 %cholesky.468 = f32[128,128]{1,0:T(8,128)S(1)} custom-call(f32[128,128]{1,0:T(8,128)S(1)} %cholesky.589), custom_call_target="Cholesky" | custom-call | tf_op jit(solution)/shard_map/jit(cholesky)/cholesky | solution.py:47
  545.2 9.8 %custom-call.64 = f32[1,128,128]{1,2,0:T(8,128)S(1)} custom-call(f32[1,128,128]{2,1,0:T(8,128)S(1)} %get-tuple-element.69), custom_call_target="InvertDiagBlocksLowerTriangular" | custom-call | tf_op jit(solution)/shard_map/jit(cholesky)/cholesky | solution.py:47
  555.0 1.2 convolution_dynamic-update-slice_fusion.2
  556.2 2.3 convolution_subtract_fusion.7
  558.5 12.1 %cholesky.487 = f32[128,128]{1,0:T(8,128)S(1)} custom-call(f32[128,128]{1,0:T(8,128)S(1)} %cholesky.594), custom_call_target="Cholesky" | custom-call | tf_op jit(solution)/shard_map/jit(cholesky)/cholesky | solution.py:47
  571.9 9.8 %custom-call.65 = f32[1,128,128]{1,2,0:T(8,128)S(1)} custom-call(f32[1,128,128]{2,1,0:T(8,128)S(1)} %get-tuple-element.66), custom_call_target="InvertDiagBlocksLowerTriangular" | custom-call | tf_op jit(solution)/shard_map/jit(cholesky)/cholesky | solution.py:47
  581.8 1.1 convolution_dynamic-update-slice_fusion.3
  582.9 2.3 convolution_subtract_fusion.8
  585.2 11.7 %cholesky.506 = f32[128,128]{1,0:T(8,128)S(1)} custom-call(f32[128,128]{1,0:T(8,128)S(1)} %cholesky.599), custom_call_target="Cholesky" | custom-call | tf_op jit(solution)/shard_map/jit(cholesky)/cholesky | solution.py:47
  598.2 10.0 %custom-call.66 = f32[1,128,128]{1,2,0:T(8,128)S(1)} custom-call(f32[1,128,128]{2,1,0:T(8,128)S(1)} %get-tuple-element.63), custom_call_target="InvertDiagBlocksLowerTriangular" | custom-call | tf_op jit(solution)/shard_map/jit(cholesky)/cholesky | solution.py:47
  608.2 1.0 convolution_dynamic-update-slice_fusion.4
  609.2 2.3 convolution_subtract_fusion.9
  611.5 11.7 %cholesky.526 = f32[128,128]{1,0:T(8,128)S(1)} custom-call(f32[128,128]{1,0:T(8,128)S(1)} %cholesky.604), custom_call_target="Cholesky" | custom-call | tf_op jit(solution)/shard_map/jit(cholesky)/cholesky | solution.py:47
  624.5 9.8 %custom-call.67 = f32[1,128,128]{1,2,0:T(8,128)S(1)} custom-call(f32[1,128,128]{2,1,0:T(8,128)S(1)} %get-tuple-element.60), custom_call_target="InvertDiagBlocksLowerTriangular" | custom-call | tf_op jit(solution)/shard_map/jit(cholesky)/cholesky | solution.py:47
  634.3 0.9 convolution_dynamic-update-slice_fusion.5
  635.2 2.0 convolution_subtract_fusion.10
  637.3 11.9 %cholesky.546 = f32[128,128]{1,0:T(8,128)S(1)} custom-call(f32[128,128]{1,0:T(8,128)S(1)} %cholesky.609), custom_call_target="Cholesky" | custom-call | tf_op jit(solution)/shard_map/jit(cholesky)/cholesky | solution.py:47
  650.4 9.8 %custom-call.68 = f32[1,128,128]{1,2,0:T(8,128)S(1)} custom-call(f32[1,128,128]{2,1,0:T(8,128)S(1)} %get-tuple-element.57), custom_call_target="InvertDiagBlocksLowerTriangular" | custom-call | tf_op jit(solution)/shard_map/jit(cholesky)/cholesky | solution.py:47
  661.1 1.8 convolution_subtract_fusion.12
  662.9 11.7 %cholesky.564 = f32[128,128]{1,0:T(8,128)S(1)} custom-call(f32[128,128]{1,0:T(8,128)S(1)} %convolution_subtract_fusion.12), custom_call_target="Cholesky" | custom-call | tf_op jit(solution)/shard_map/jit(cholesky)/cholesky | solution.py:47
  681.5 6.7 fusion.1
  688.2 23.6 %while.1 = (s32[]{:T(128)}, f32[1024,1024]{1,0:T(8,128)}, s32[8,2]{0,1:T(2,128)S(1)}, f32[8,128,128]{2,1,0:T(8,128)S(1)}, s32[]{:T(128)}) while((s32[]{:T(128)}, f32[1024,1024]{1,0:T(8,128)}, s32[8,2]{0,1:T(2,128)S(1)}, f32[8,128,128]{2,1,0:T(8,128)S(1)}, s32[]{:T(128)}) %tuple.59), condition=%wide.while_cond, body=%wide.while_body.sunk | while | flops 2 | bytes 131189 | solution.py:48
  688.8 2.3 bitcast_dynamic-update-slice_fusion.2
  691.8 2.3 bitcast_dynamic-update-slice_fusion.2
  694.7 2.3 bitcast_dynamic-update-slice_fusion.2
  697.7 2.3 bitcast_dynamic-update-slice_fusion.2
  700.6 2.3 bitcast_dynamic-update-slice_fusion.2
  703.6 2.3 bitcast_dynamic-update-slice_fusion.2
  706.6 2.3 bitcast_dynamic-update-slice_fusion.2
  709.5 2.2 bitcast_dynamic-update-slice_fusion.2
  711.7 79.0 %custom-call.69 = f32[8,128,128]{1,2,0:T(8,128)S(1)} custom-call(f32[8,128,128]{2,1,0:T(8,128)S(1)} %get-tuple-element.12), custom_call_target="InvertDiagBlocksLowerTriangular" | custom-call | tf_op jit(solution)/shard_map/triangular_solve | solution.py:48
  791.3 1.9 convolution_subtract_fusion.4
  794.0 1.6 convolution_subtract_fusion
  796.3 2.0 fusion.16
  799.1 2.2 fusion.19
  802.1 2.6 convolution_subtract_fusion.2
  805.4 2.8 convolution_subtract_fusion.1
  808.9 3.4 convolution_subtract_fusion.3
  813.0 4.4 fusion.78
  819.1 132.4 %all-reduce.4.cloned.1.call-done = (f32[64,1024]{1,0:T(8,128)}, f32[64,1024]{1,0:T(8,128)}) async-done(((f32[64,1024]{1,0:T(8,128)}, f32[64,1024]{1,0:T(8,128)}), (f32[64,1024]{1,0:T(8,128)}, f32[64,1024]{1,0:T(8,128)})) %all-reduce.4.cloned.1.call-update) | async-done | bytes 524304 | tf_op jit(solution)/shard_map/psum | solution.py:12
  951.5 1.8 fusion.22
  (75 shorter events, 24.3 us)
Async XLA Ops:
  6.5 165.4 %all-gather.5.cloned.1.call-start = ((), (), s32[]{:S(2)}) async-start(), calls=%async_computation.1 | async-start | bytes 4325376 | tf_op jit(solution)/shard_map/all_gather | solution.py:25
  7.3 241.4 %reduce-scatter.2.cloned.1.call-start = ((), (), s32[]{:S(2)}) async-start(), calls=%async_computation.2 | async-start | bytes 2228224 | tf_op jit(solution)/shard_map/reduce_scatter | solution.py:30
  175.4 73.2 %copy-start.3 = (f32[128]{0:T(128)S(1)}, f32[128]{0:T(128)}, u32[]{:S(2)}) copy-start(f32[128]{0:T(128)} %param.3) | copy-start | bytes 1540
  177.0 233.6 %all-gather.7.cloned.1.call-start = ((), (), s32[]{:S(2)}) async-start(), calls=%async_computation.3 | async-start | bytes 4325376 | tf_op jit(solution)/shard_map/all_gather | solution.py:44
  250.3 210.1 %all-gather.9.cloned.1.call-start = ((), (), s32[]{:S(2)}) async-start(), calls=%async_computation.4 | async-start | bytes 4456448 | tf_op jit(solution)/shard_map/all_gather | solution.py:46
  412.5 539.0 %all-reduce.4.cloned.1.call-start = ((), (), s32[]{:S(2)}) async-start(), calls=%async_computation.5 | async-start | bytes 1048576 | tf_op jit(solution)/shard_map/psum | solution.py:12
  476.5 2.0 copy-start.1
  790.7 3.2 copy-start
  812.3 5.9 copy-start.2
Sparse Core Ops, SparseCore 0:
  10.5 161.4 all-gather.4
  177.1 71.4 reduce-scatter.1
  251.5 158.9 all-gather.6
  412.6 47.7 all-gather.8
  818.4 133.0 all-reduce.3
where the time goes:
time: 965 us; the launch traced here: 961 us
  waiting for transfers between devices  573 us (59%)
  other arithmetic  270 us (28%)
  matrix products  54.9 us (6%)
  local copies, waits for them, and re-layouts  43.6 us (5%)
  between operations  18.7 us (2%)
    another operation x30, other arithmetic, body(): lower_factor = jnp.linalg.cholesky(diagonal)  172 us
    all_gather x1, waiting for transfers between devices, body(): everyone = lax.all_gather(interactions, 'col', axis=0, tiled=True)  165 us
    all_gather x1, waiting for transfers between devices, body(): row_band = lax.all_gather(grid_tile, 'col', axis=2, tiled=True)  160 us
    psum x1, waiting for transfers between devices, from_root(): return lax.psum(kept, axis)  132 us
    another operation x3, other arithmetic, body(): lax.linalg.triangular_solve(lower_factor, jnp.eye(PANEL, dtype=jnp.float3...  85.7 us
    reduce_scatter x1, waiting for transfers between devices, body(): lax.psum_scatter(term_block.reshape(per_owner * lax.axis_size('row'), blo...  71.5 us
    all_gather x1, waiting for transfers between devices, body(): diagonal = lax.all_gather(corner, 'row', axis=0, tiled=True)  43.8 us
    another operation x24, local copies, waits for them, and re-layouts  23.4 us
  transfers between devices with their start and end apart: 5, of which 5 were waited for; matrix products, arithmetic and copies ran while one was open for 0% of the time, Pallas kernels for 0%

commit v1 on v0

v1 whole, which is shorter than its diff:
```python
import functools
import jax
import jax.numpy as jnp
from jax import lax
from jax.experimental import pallas as pl
from jax.experimental.pallas import tpu as pltpu
from jax.sharding import PartitionSpec as P

PANEL = 1024
SPAN = 4
HI = lax.Precision.HIGHEST


def bl(x, lane):
    return jnp.broadcast_to(x[:, lane:lane+1], (8, 128))
def bs(x, row):
    return jnp.broadcast_to(x[row:row+1, :], (8, 128))

def factor(S, E):
    sub = lax.broadcasted_iota(jnp.int32, (8, 128), 0)
    U, V = [], []
    n = len(S)
    S = list(S); E = list(E)
    for b in range(n):
        C = [bl(S[b], 8*b+i) for i in range(8)]
        s = {}
        for i in range(8):
            for t in range(i, 8):
                s[t, i] = bs(C[i], t)
        R = [bs(S[b], i) for i in range(8)]
        Q = [bs(E[b], i) for i in range(8)]
        rd, l = [], {}
        for i in range(8):
            rd.append(1.0 / s[i, i])
            for t in range(i+1, 8):
                l[t, i] = s[t, i] * rd[i]
            for u in range(i+1, 8):
                for t in range(u, 8):
                    s[t, u] = s[t, u] - l[t, i] * s[u, i]
            for t in range(i+1, 8):
                R[t] = R[t] - l[t, i] * R[i]
                Q[t] = Q[t] - l[t, i] * Q[i]
        ru = [lax.rsqrt(s[i, i]) for i in range(8)]
        Uo = R[0] * ru[0]; Vo = Q[0] * ru[0]
        for i in range(1, 8):
            Uo = jnp.where(sub == i, R[i] * ru[i], Uo)
            Vo = jnp.where(sub == i, Q[i] * ru[i], Vo)
        U.append(Uo); V.append(Vo)
        if b == n-1: break
        Z = [None]*8; Y = [None]*8
        for i in range(7, -1, -1):
            z = R[i] * rd[i]; y = Q[i] * rd[i]
            for t in range(7, i, -1):
                z = z - l[t, i] * Z[t]
                y = y - l[t, i] * Y[t]
            Z[i] = z; Y[i] = y
        for g in range(b+1, n):
            c = [bl(S[g], 8*b+i) for i in range(8)]
            a0 = c[0]*Z[0]; a1 = c[1]*Z[1]; e0 = c[0]*Y[0]; e1 = c[1]*Y[1]
            for i in range(2, 8, 2):
                a0 = a0 + c[i]*Z[i]; a1 = a1 + c[i+1]*Z[i+1]
                e0 = e0 + c[i]*Y[i]; e1 = e1 + c[i+1]*Y[i+1]
            S[g] = S[g] - (a0 + a1)
            E[g] = E[g] - (e0 + e1)
    return U, V

def dt(a, b):
    return lax.dot_general(a, b, (((1,), (1,)), ((), ())), precision=HI, preferred_element_type=jnp.float32)

def k2(r, c, m_ref, tile_ref, out_ref, L, B, T, *, look):
    lane = lax.broadcasted_iota(jnp.int32, (8, 128), 1)
    sub = lax.broadcasted_iota(jnp.int32, (8, 128), 0)
    E0 = [jnp.where(lane == sub + 8*g, 1.0, 0.0).astype(jnp.float32) for g in range(16)]
    R = m_ref.shape[0]
    B[...] = m_ref[:, :128]
    for J in range(8):
        j0 = 128*J; r0 = j0 + 128
        S = [B[pl.ds(j0 + 8*g, 8), :] for g in range(16)]
        U, V = factor(S, E0)
        if J < 7 and look:
            if J == 0:
                T[pl.ds(r0, R-r0), :] = m_ref[pl.ds(r0, R-r0), pl.ds(r0, 128)]
            else:
                T[pl.ds(r0, R-r0), :] = m_ref[pl.ds(r0, R-r0), pl.ds(r0, 128)] - dt(L[pl.ds(r0, R-r0), pl.ds(0, j0)], L[pl.ds(r0, 128), pl.ds(0, j0)])
        Um = jnp.concatenate([jnp.where(lane >= sub + 8*g, U[g], 0.0) for g in range(16)], 0)
        Vm = jnp.concatenate(V, 0)
        L[pl.ds(j0, 128), pl.ds(j0, 128)] = Um.T
        if look:
            Pn = dt(B[pl.ds(r0, 128), :], Vm)
            L[pl.ds(r0, 128), pl.ds(j0, 128)] = Pn
            if J < 7:
                Bn = T[pl.ds(r0, 128), :] - dt(Pn, Pn)
                r1 = r0 + 128
                Pr = dt(B[pl.ds(r1, R-r1), :], Vm)
                L[pl.ds(r1, R-r1), pl.ds(j0, 128)] = Pr
                B[pl.ds(r0, 128), :] = Bn
                B[pl.ds(r1, R-r1), :] = T[pl.ds(r1, R-r1), :] - dt(Pr, Pn)
            else:
                r1 = r0 + 128
                L[pl.ds(r1, R-r1), pl.ds(j0, 128)] = dt(B[pl.ds(r1, R-r1), :], Vm)
        else:
            L[pl.ds(r0, R-r0), pl.ds(j0, 128)] = dt(B[pl.ds(r0, R-r0), :], Vm)
            if J < 7:
                B[pl.ds(r0, R-r0), :] = m_ref[pl.ds(r0, R-r0), pl.ds(r0, 128)] - dt(L[pl.ds(r0, R-r0), pl.ds(0, r0)], L[pl.ds(r0, 128), pl.ds(0, r0)])
    for J in range(7):
        L[pl.ds(128*J, 128), pl.ds(128*(J+1), 128*(7-J))] = jnp.zeros((128, 128*(7-J)), jnp.float32)
    tr = tile_ref[1:].reshape(192, 128) - dt(L[pl.ds(1024, 192), :], L[pl.ds(1216, 128), :])
    cc = jnp.minimum(c, 7)
    col = pl.multiple_of(cc*128, 128)
    first = L[pl.ds(pl.multiple_of(r*64, 64), 64), pl.ds(col, 128)]
    lt = L[pl.ds(1024, 192), pl.ds(col, 128)]
    inp = c < 8
    out_ref[0] = jnp.where(inp, first, 0.0)
    out_ref[1:] = jnp.where(inp, lt, tr).reshape(3, 64, 128)


def finish_kernel(m_ref, tile_ref, out_ref, L, B, T):
    k2(lax.axis_index("row"), lax.axis_index("col"), m_ref, tile_ref, out_ref, L, B, T, look=True)


def finish(m, tile):
    rows = m.shape[0]
    return pl.pallas_call(
        finish_kernel,
        out_shape=jax.ShapeDtypeStruct(tile.shape, jnp.float32),
        scratch_shapes=[
            pltpu.VMEM((rows, PANEL), jnp.float32),
            pltpu.VMEM((rows, 128), jnp.float32),
            pltpu.VMEM((rows, 128), jnp.float32),
        ],
        compiler_params=pltpu.CompilerParams(vmem_limit_bytes=50 * 1024 * 1024),
        name="finish",
    )(m, tile)


def body(interactions, regular):
    row_count = lax.axis_size("row")
    row_index = lax.axis_index("row")
    col_index = lax.axis_index("col")
    block_width = interactions.shape[0]
    user_count = interactions.shape[1]
    band_rows = PANEL // row_count
    per_owner = SPAN * band_rows
    everyone = lax.all_gather(interactions, "col", axis=0, tiled=True)
    grouped = everyone.reshape(SPAN, row_count, band_rows, user_count)
    term_block = jnp.einsum(
        "kotu,ju->oktj", grouped, interactions, preferred_element_type=jnp.float32
    )
    grid_tile = lax.psum_scatter(
        term_block.reshape(per_owner * row_count, block_width),
        "row",
        scatter_dimension=0,
        tiled=True,
    ).reshape(SPAN, band_rows, block_width)
    row_items = (
        jnp.arange(SPAN, dtype=jnp.int32)[:, None] * PANEL
        + row_index * band_rows
        + jnp.arange(band_rows, dtype=jnp.int32)[None, :]
    )
    col_items = col_index * block_width + jnp.arange(block_width, dtype=jnp.int32)
    on_diagonal = row_items[:, :, None] == col_items[None, None, :]
    grid_tile = grid_tile + jnp.where(on_diagonal, regular[None, None, :], jnp.float32(0.0))
    row_band = lax.all_gather(grid_tile, "col", axis=2, tiled=True)[:, :, :PANEL]
    diagonal = lax.all_gather(row_band[0], "row", axis=0, tiled=True)
    mcols = lax.all_gather(grid_tile[0], "row", axis=0, tiled=True).T
    m = jnp.concatenate([diagonal, row_band[1:].reshape(3 * band_rows, PANEL), mcols], 0)
    return finish(m, grid_tile)


def solution(mesh):
    return jax.shard_map(
        body,
        mesh=mesh,
        in_specs=(P("col", "row"), P("col")),
        out_specs=P(None, "row", "col"),
        check_vma=False,
    )
```

time: 965 us -> 535 us (0.55)
  other arithmetic: 270 us -> 7.29 us
  waiting for transfers between devices: 573 us -> 414 us
  matrix products: 54.9 us -> 3.52 us
  Pallas kernels: 0 us -> 51.2 us
  local copies, waits for them, and re-layouts: 43.6 us -> 5.29 us
  blocking collectives: 0 us -> 29.3 us
    another operation x33 -> x0, other arithmetic: 258 us -> none  [the longest x30 172 us: body(): lower_factor = jnp.linalg.cholesky(diagonal)]
    psum x1 -> x0, waiting for transfers between devices: 132 us -> none  [from_root(): return lax.psum(kept, axis)]
    pallas_call x0 -> x1, Pallas kernels: none -> 51.2 us  [finish(): pl.pallas_call(finish_kernel, out_shape=jax.ShapeDtypeStruct(tile.shape,...]
    another operation x29 -> x0, matrix products: 45.2 us -> none  [the longest x14 23.1 us: body(): lower_factor = jnp.linalg.cholesky(diagonal)]
    all_gather x0 -> x1, blocking collectives: none -> 29.3 us  [body(): mcols = lax.all_gather(grid_tile[0], 'row', axis=0, tiled=True).T]
    all_gather x2, waiting for transfers between devices: 204 us -> 178 us  [the longest x1 160 us: body(): lax.all_gather(grid_tile, 'col', axis=2, tiled=True)[:, :, :PANEL]]
    another operation x33 -> x0, local copies, waits for them, and re-layouts: 25.9 us -> none
    all_gather x1 -> x0, local copies, waits for them, and re-layouts: 11.1 us -> none  [body(): diagonal = lax.all_gather(corner, 'row', axis=0, tiled=True)]
  transfers between devices with their start and end apart: 5 -> 4, of which waited for: 5 -> 4; matrix products, arithmetic and copies ran while one was open for 0% -> 0% of each run, Pallas kernels for 0% -> 0%
where the time goes in v1:
time: 535 us; the launch traced here: 525 us
  waiting for transfers between devices  414 us (77%)
  Pallas kernels  51.2 us (10%)
  blocking collectives  29.3 us (5%)
  between operations  13.6 us (3%)
  other arithmetic  7.29 us (1%)
    all_gather x1, waiting for transfers between devices, body(): everyone = lax.all_gather(interactions, 'col', axis=0, tiled=True)  165 us
    all_gather x1, waiting for transfers between devices, body(): lax.all_gather(grid_tile, 'col', axis=2, tiled=True)[:, :, :PANEL]  160 us
    reduce_scatter x1, waiting for transfers between devices, body(): lax.psum_scatter(term_block.reshape(per_owner * row_count, block_width),...  71.4 us
    pallas_call x1, Pallas kernels, finish(): pl.pallas_call(finish_kernel, out_shape=jax.ShapeDtypeStruct(tile.shape,...  51.2 us
    all_gather x1, blocking collectives, body(): mcols = lax.all_gather(grid_tile[0], 'row', axis=0, tiled=True).T  29.3 us
    all_gather x1, waiting for transfers between devices, body(): diagonal = lax.all_gather(row_band[0], 'row', axis=0, tiled=True)  17.3 us
  transfers between devices with their start and end apart: 4, of which 4 were waited for; matrix products, arithmetic and copies ran while one was open for 0% of the time, Pallas kernels for 0%

profile of v1, /device:TPU:1, one launch (start us, length us, event | category | flops | bytes accessed | tf_op | source)
XLA Modules:
  0.0 524.7 jit_solution(4981136319074668960)
XLA Ops:
  6.5 0.0 all-gather.6.cloned.1.call-start
  6.5 0.7 all-gather.6.cloned.1.call-update
  7.3 0.0 reduce-scatter.2.cloned.1.call-start
  7.3 164.6 %all-gather.6.cloned.1.call-done = bf16[4096,512]{1,0:T(8,128)(2,1)} async-done(((bf16[128,512]{1,0:T(8,128)(2,1)}), bf16[4096,512]{1,0:T(8,128)(2,1)}) %all-gather.6.cloned.1.call-update) | async-done | bytes 4194320 | tf_op jit(solution)/shard_map/all_gather | solution.py:144
  171.9 3.5 convolution_bitcast_fusion
  175.4 0.0 copy-start.1
  175.4 1.5 copy.4
  176.9 0.0 reduce-scatter.2.cloned.1.call-update
  176.9 0.0 all-gather.8.cloned.1.call-start
  177.0 0.1 iota_add_fusion
  177.1 71.4 %reduce-scatter.2.cloned.1.call-done = f32[256,128]{1,0:T(8,128)} async-done(((f32[4096,128]{1,0:T(8,128)}), f32[256,128]{1,0:T(8,128)}) %reduce-scatter.2.cloned.1.call-update) | async-done | bytes 131088 | tf_op jit(solution)/shard_map/reduce_scatter | solution.py:149
  248.5 0.0 copy-done.1
  248.5 1.7 select_add_fusion.tile_ref
  250.2 0.0 all-gather.8.cloned.1.call-update
  250.2 0.0 all-gather.10.cloned.1.call-start
  250.3 160.3 %all-gather.8.cloned.1.call-done = f32[4,64,4096]{2,1,0:T(8,128)} async-done(((f32[4,64,128]{2,1,0:T(8,128)}), f32[4,64,4096]{2,1,0:T(8,128)}) %all-gather.8.cloned.1.call-update) | async-done | bytes 4194320 | tf_op jit(solution)/shard_map/all_gather | solution.py:163
  410.6 1.7 slice.15
  412.2 0.0 all-gather.10.cloned.1.call-update
  412.3 0.8 slice.17
  413.0 29.3 %all-gather.1 = f32[1,1024,128]{2,1,0:T(8,128)S(1)} all-gather(f32[1,64,128]{2,1,0:T(8,128)S(1)} %slice.17), channel_id=3, replica_groups=mesh['row'=16,'col'=32] {'row'}, dimensions={1}, use_global_device_ids=true | all-gather | bytes 557056 | tf_op jit(solution)/shard_map/all_gather | solution.py:165
  442.4 0.2 copy.5
  442.6 1.2 slice.16
  443.8 17.3 %all-gather.10.cloned.1.call-done = f32[1,1024,1024]{2,1,0:T(8,128)} async-done(((f32[1,64,1024]{2,1,0:T(8,128)}), f32[1,1024,1024]{2,1,0:T(8,128)}) %all-gather.10.cloned.1.call-update) | async-done | bytes 4194320 | tf_op jit(solution)/shard_map/all_gather | solution.py:164
  461.1 0.0 copy-start
  461.1 5.5 %pad_maximum_fusion.m_ref = f32[1344,1024]{1,0:T(8,128)} fusion(f32[128,1024]{1,0:T(8,128)S(1)} %copy.5, f32[192,1024]{1,0:T(8,128)S(1)} %bitcast.19, f32[1024,1024]{1,0:T(8,128)} %bitcast.17), kind=kLoop, calls=%fused_computation | loop fusion | flops 2752512 | bytes 11010048 | tf_op jit(solution)/shard_map/concatenate | solution.py:166
  466.6 0.0 copy-done
  466.6 51.2 %finish.1 = f32[4,64,128]{2,1,0:T(8,128)} custom-call(f32[1344,1024]{1,0:T(8,128)} %pad_maximum_fusion.m_ref, f32[4,64,128]{2,1,0:T(8,128)S(1)} %copy-done), custom_call_target="tpu_custom_call" | custom-call | tf_op jit(solution)/shard_map/finish/pallas_call | solution.py:123
  (2 shorter events, 0.0 us)
Async XLA Ops:
  6.5 165.4 %all-gather.6.cloned.1.call-start = ((), (), s32[]{:S(2)}) async-start(), calls=%async_computation.1 | async-start | bytes 4325376 | tf_op jit(solution)/shard_map/all_gather | solution.py:144
  7.3 241.3 %reduce-scatter.2.cloned.1.call-start = ((), (), s32[]{:S(2)}) async-start(), calls=%async_computation.2 | async-start | bytes 2228224 | tf_op jit(solution)/shard_map/reduce_scatter | solution.py:149
  175.4 73.1 %copy-start.1 = (f32[128]{0:T(128)S(1)}, f32[128]{0:T(128)}, u32[]{:S(2)}) copy-start(f32[128]{0:T(128)} %param.3) | copy-start | bytes 1540
  176.9 233.6 %all-gather.8.cloned.1.call-start = ((), (), s32[]{:S(2)}) async-start(), calls=%async_computation.3 | async-start | bytes 4325376 | tf_op jit(solution)/shard_map/all_gather | solution.py:163
  250.2 210.8 %all-gather.10.cloned.1.call-start = ((), (), s32[]{:S(2)}) async-start(), calls=%async_computation.4 | async-start | bytes 4456448 | tf_op jit(solution)/shard_map/all_gather | solution.py:164
  461.1 5.5 %copy-start = (f32[4,64,128]{2,1,0:T(8,128)S(1)}, f32[4,64,128]{2,1,0:T(8,128)}, u32[]{:S(2)}) copy-start(f32[4,64,128]{2,1,0:T(8,128)} %select_add_fusion.tile_ref) | copy-start | bytes 393220
Sparse Core Ops, SparseCore 0:
  10.5 161.3 all-gather.5
  177.0 71.4 reduce-scatter.1
  251.4 159.0 all-gather.7
  412.6 48.4 all-gather.9

commit v2 on v1

v2 whole, which is shorter than its diff:
```python
import jax
import jax.numpy as jnp
from jax import lax
from jax.experimental import pallas as pl
from jax.experimental.pallas import tpu as pltpu
from jax.sharding import PartitionSpec as P

PANEL = 1024
RING = 16
HI = lax.Precision.HIGHEST
MESH = pl.DeviceIdType.MESH


def gather_kernel(x_ref, reg_ref, tile_ref, band_ref, xg, wc, prod, parts, halves,
                  ring_send, ring_recv, pair_send, pair_recv, part_send, part_recv, panel_send, panel_recv):
    r = lax.axis_index("row")
    c = lax.axis_index("col")
    h = c // RING
    z = c % RING
    other = 1 - h
    chip = r // 2
    core = r % 2
    right = h * RING + (z + 1) % RING
    left = h * RING + (z + RING - 1) % RING
    partner = other * RING + z

    barrier = pltpu.get_barrier_semaphore()
    for near in (left, right, partner):
        pl.semaphore_signal(barrier, inc=1, device_id=(r, near), device_id_type=MESH)
    for step in range(1, 16):
        pl.semaphore_signal(barrier, inc=1, device_id=((r + step) % 16, c), device_id_type=MESH)
    pl.semaphore_wait(barrier, 18)

    def remote(src, dst, send, recv, device):
        return pltpu.make_async_remote_copy(
            src_ref=src, dst_ref=dst, send_sem=send, recv_sem=recv, device_id=device, device_id_type=MESH
        )

    swap = remote(x_ref, wc.at[h], pair_send.at[0], pair_recv.at[0], (r, partner))
    swap.start()

    def ring_copy(way, step, half):
        owner = (z - step + 1 + RING) % RING if way == 0 else (z + step - 1) % RING
        rows = pl.ds(64 * half, 64)
        src = x_ref.at[rows] if step == 1 else xg.at[owner, rows]
        return remote(src, xg.at[owner, rows], ring_send.at[way, step - 1, half],
                      ring_recv.at[way, step - 1, half], (r, right if way == 0 else left))

    steps = (8, 7)
    for half in range(2):
        for way in range(2):
            ring_copy(way, 1, half).start()
    wc[h] = x_ref[...]

    def multiply(owner, block):
        both = wc[...].reshape(256, 512)
        product = lax.dot_general(block, both, (((1,), (1,)), ((), ())), preferred_element_type=jnp.float32)
        prod[owner] = product.reshape(2, 64, 256)
        place = owner % 8
        half_k = owner // 8
        for to in range(2):
            mine = jnp.logical_and(place == chip, core == to)

            @pl.when(jnp.logical_not(mine))
            def _():
                remote(prod.at[owner, to], parts.at[half_k, r], part_send, part_recv.at[half_k],
                       (2 * place + to, c)).start()

            @pl.when(mine)
            def _():
                parts[half_k, r] = prod[owner, to]

    swap.wait()
    multiply(z, x_ref[...])
    for step in range(1, 9):
        for half in range(2):
            for way in range(2):
                if step <= steps[way]:
                    ring_copy(way, step, half).wait_recv()
                    if step < steps[way]:
                        ring_copy(way, step + 1, half).start()
        for way in range(2):
            if step <= steps[way]:
                owner = (z - step + RING) % RING if way == 0 else (z + step) % RING
                multiply(owner, xg[owner])

    lane = lax.broadcasted_iota(jnp.int32, (64, 128), 1)
    sub = lax.broadcasted_iota(jnp.int32, (64, 128), 0)
    for half_k in range(2):
        pltpu.make_async_copy(parts.at[half_k, pl.ds(0, 15)], parts.at[half_k, pl.ds(0, 15)], part_recv.at[half_k]).wait()
        total = parts[half_k, 0]
        for source in range(1, 16):
            total = total + parts[half_k, source]
        for side in range(2):
            block = total[:, 128 * side:128 * side + 128]
            hit = jnp.logical_and(chip + 8 * half_k == z, h == side)
            diagonal = jnp.logical_and(lane == sub + 64 * core, hit)
            halves[side, half_k] = block + jnp.where(diagonal, jnp.broadcast_to(reg_ref[...], (64, 128)), 0.0)

    give = remote(halves.at[other], tile_ref.at[pl.ds(2 * h, 2)], pair_send.at[1], pair_recv.at[1], (r, partner))
    give.start()
    tile_ref[pl.ds(2 * h, 2)] = halves[h]
    in_panel = z < 8
    lend = remote(halves.at[0], band_ref.at[jnp.minimum(z, 7), pl.ds(0, 2)], pair_send.at[2], pair_recv.at[2], (r, partner))

    @pl.when(jnp.logical_and(in_panel, h == 0))
    def _():
        lend.start()

    @pl.when(jnp.logical_and(in_panel, h == 1))
    def _():
        band_ref[z, pl.ds(2, 2)] = halves[0]
        lend.wait_recv()

    give.wait()

    @pl.when(jnp.logical_and(in_panel, h == 0))
    def _():
        band_ref[z] = tile_ref[...]
        lend.wait_send()

    def panel_copy(way, step):
        owner = (z - step + 1 + RING) % RING if way == 0 else (z + step - 1) % RING
        slot = jnp.minimum(owner, 7)
        return owner < 8, remote(band_ref.at[slot], band_ref.at[slot], panel_send.at[way, step - 1],
                                 panel_recv.at[way, step - 1], (r, right if way == 0 else left))

    def panel_arrival(way, step):
        owner = (z - step + RING) % RING if way == 0 else (z + step) % RING
        slot = jnp.minimum(owner, 7)
        return owner < 8, remote(band_ref.at[slot], band_ref.at[slot], panel_send.at[way, step - 1],
                                 panel_recv.at[way, step - 1], (r, right if way == 0 else left))

    for step in range(1, 9):
        for way in range(2):
            if step <= steps[way]:
                if step > 1:
                    here, copy = panel_arrival(way, step - 1)
                    pl.when(here)(copy.wait_recv)
                here, copy = panel_copy(way, step)
                pl.when(here)(copy.start)
    for way in range(2):
        here, copy = panel_arrival(way, steps[way])
        pl.when(here)(copy.wait_recv)
    for way in range(2):
        for step in range(1, steps[way] + 1):
            here, copy = panel_copy(way, step)
            pl.when(here)(copy.wait_send)
            for half in range(2):
                ring_copy(way, step, half).wait_send()
    pltpu.make_async_copy(prod.at[pl.ds(0, 15)], prod.at[pl.ds(0, 15)], part_send).wait()


def gather(interactions, regular):
    vmem = pl.BlockSpec(memory_space=pltpu.VMEM)
    return pl.pallas_call(
        gather_kernel,
        out_shape=[
            jax.ShapeDtypeStruct((4, 64, 128), jnp.float32),
            jax.ShapeDtypeStruct((8, 4, 64, 128), jnp.float32),
        ],
        in_specs=[vmem, vmem],
        out_specs=[vmem, vmem],
        scratch_shapes=[
            pltpu.VMEM((RING, 128, 512), jnp.bfloat16),
            pltpu.VMEM((2, 128, 512), jnp.bfloat16),
            pltpu.VMEM((RING, 2, 64, 256), jnp.float32),
            pltpu.VMEM((2, 16, 64, 256), jnp.float32),
            pltpu.VMEM((2, 2, 64, 128), jnp.float32),
            pltpu.SemaphoreType.DMA((2, 8, 2)),
            pltpu.SemaphoreType.DMA((2, 8, 2)),
            pltpu.SemaphoreType.DMA((3,)),
            pltpu.SemaphoreType.DMA((3,)),
            pltpu.SemaphoreType.DMA,
            pltpu.SemaphoreType.DMA((2,)),
            pltpu.SemaphoreType.DMA((2, 8)),
            pltpu.SemaphoreType.DMA((2, 8)),
        ],
        compiler_params=pltpu.CompilerParams(
            collective_id=0, has_side_effects=True, vmem_limit_bytes=50 * 1024 * 1024
        ),
        name="gather",
    )(interactions, regular.reshape(1, 128))


def bl(x, lane):
    return jnp.broadcast_to(x[:, lane:lane+1], (8, 128))
def bs(x, row):
    return jnp.broadcast_to(x[row:row+1, :], (8, 128))

def factor(S, E):
    sub = lax.broadcasted_iota(jnp.int32, (8, 128), 0)
    U, V = [], []
    n = len(S)
    S = list(S); E = list(E)
    for b in range(n):
        C = [bl(S[b], 8*b+i) for i in range(8)]
        s = {}
        for i in range(8):
            for t in range(i, 8):
                s[t, i] = bs(C[i], t)
        R = [bs(S[b], i) for i in range(8)]
        Q = [bs(E[b], i) for i in range(8)]
        rd, l = [], {}
        for i in range(8):
            rd.append(1.0 / s[i, i])
            for t in range(i+1, 8):
                l[t, i] = s[t, i] * rd[i]
            for u in range(i+1, 8):
                for t in range(u, 8):
                    s[t, u] = s[t, u] - l[t, i] * s[u, i]
            for t in range(i+1, 8):
                R[t] = R[t] - l[t, i] * R[i]
                Q[t] = Q[t] - l[t, i] * Q[i]
        ru = [lax.rsqrt(s[i, i]) for i in range(8)]
        Uo = R[0] * ru[0]; Vo = Q[0] * ru[0]
        for i in range(1, 8):
            Uo = jnp.where(sub == i, R[i] * ru[i], Uo)
            Vo = jnp.where(sub == i, Q[i] * ru[i], Vo)
        U.append(Uo); V.append(Vo)
        if b == n-1: break
        Z = [None]*8; Y = [None]*8
        for i in range(7, -1, -1):
            z = R[i] * rd[i]; y = Q[i] * rd[i]
            for t in range(7, i, -1):
                z = z - l[t, i] * Z[t]
                y = y - l[t, i] * Y[t]
            Z[i] = z; Y[i] = y
        for g in range(b+1, n):
            c = [bl(S[g], 8*b+i) for i in range(8)]
            a0 = c[0]*Z[0]; a1 = c[1]*Z[1]; e0 = c[0]*Y[0]; e1 = c[1]*Y[1]
            for i in range(2, 8, 2):
                a0 = a0 + c[i]*Z[i]; a1 = a1 + c[i+1]*Z[i+1]
                e0 = e0 + c[i]*Y[i]; e1 = e1 + c[i+1]*Y[i+1]
            S[g] = S[g] - (a0 + a1)
            E[g] = E[g] - (e0 + e1)
    return U, V


def dt(a, b):
    return lax.dot_general(a, b, (((1,), (1,)), ((), ())), precision=HI, preferred_element_type=jnp.float32)


def finish_kernel(m_ref, band_ref, tile_ref, out_ref, L, B, T):
    r = lax.axis_index("row")
    c = lax.axis_index("col")
    lane = lax.broadcasted_iota(jnp.int32, (8, 128), 1)
    sub = lax.broadcasted_iota(jnp.int32, (8, 128), 0)
    E0 = [jnp.where(lane == sub + 8 * g, 1.0, 0.0).astype(jnp.float32) for g in range(16)]
    R = L.shape[0]

    def pieces(J):
        above = 2 * J
        yield 128 * J, 1024 - 128 * J, m_ref[above:, J].reshape(1024 - 128 * J, 128)
        yield 1024, 192, band_ref[J, 1:].reshape(192, 128)
        yield 1216, 128, m_ref[above:above + 2, 8].reshape(128, 128).T

    for at, count, value in pieces(0):
        B[pl.ds(at, count), :] = value
    for J in range(8):
        j0 = 128 * J
        r0 = j0 + 128
        r1 = r0 + 128
        S = [B[pl.ds(j0 + 8 * g, 8), :] for g in range(16)]
        U, V = factor(S, E0)
        if J < 7:
            for at, count, value in pieces(J + 1):
                if J > 0:
                    value = value - dt(L[pl.ds(at, count), pl.ds(0, j0)], L[pl.ds(r0, 128), pl.ds(0, j0)])
                T[pl.ds(at, count), :] = value
        Um = jnp.concatenate([jnp.where(lane >= sub + 8 * g, U[g], 0.0) for g in range(16)], 0)
        Vm = jnp.concatenate(V, 0)
        L[pl.ds(j0, 128), pl.ds(j0, 128)] = Um.T
        if J < 7:
            Pn = dt(B[pl.ds(r0, 128), :], Vm)
            L[pl.ds(r0, 128), pl.ds(j0, 128)] = Pn
            Bn = T[pl.ds(r0, 128), :] - dt(Pn, Pn)
            Pr = dt(B[pl.ds(r1, R - r1), :], Vm)
            L[pl.ds(r1, R - r1), pl.ds(j0, 128)] = Pr
            B[pl.ds(r0, 128), :] = Bn
            B[pl.ds(r1, R - r1), :] = T[pl.ds(r1, R - r1), :] - dt(Pr, Pn)
        else:
            L[pl.ds(r0, R - r0), pl.ds(j0, 128)] = dt(B[pl.ds(r0, R - r0), :], Vm)
    for J in range(7):
        L[pl.ds(128 * J, 128), pl.ds(128 * (J + 1), 128 * (7 - J))] = jnp.zeros((128, 128 * (7 - J)), jnp.float32)
    tr = tile_ref[1:].reshape(192, 128) - dt(L[pl.ds(1024, 192), :], L[pl.ds(1216, 128), :])
    column = pl.multiple_of(jnp.minimum(c, 7) * 128, 128)
    first = L[pl.ds(pl.multiple_of(r * 64, 64), 64), pl.ds(column, 128)]
    solved = L[pl.ds(1024, 192), pl.ds(column, 128)]
    in_panel = c < 8
    out_ref[0] = jnp.where(in_panel, first, 0.0)
    out_ref[1:] = jnp.where(in_panel, solved, tr).reshape(3, 64, 128)


def finish(m, band, tile):
    rows = 1024 + 192 + 128
    return pl.pallas_call(
        finish_kernel,
        out_shape=jax.ShapeDtypeStruct(tile.shape, jnp.float32),
        scratch_shapes=[
            pltpu.VMEM((rows, PANEL), jnp.float32),
            pltpu.VMEM((rows, 128), jnp.float32),
            pltpu.VMEM((rows, 128), jnp.float32),
        ],
        compiler_params=pltpu.CompilerParams(vmem_limit_bytes=50 * 1024 * 1024),
        name="finish",
    )(m, band, tile)


def body(interactions, regular):
    tile, band = gather(interactions, regular)
    mine = jnp.concatenate([band[:, 0], tile[:1]], 0)
    m = lax.all_gather(mine, "row", axis=0)
    return finish(m, band, tile)


def solution(mesh):
    return jax.shard_map(
        body,
        mesh=mesh,
        in_specs=(P("col", "row"), P("col")),
        out_specs=P(None, "row", "col"),
        check_vma=False,
    )
```

time: 535 us -> 211 us (0.39); the launches traced: 525 us -> 208 us
  waiting for transfers between devices: 414 us -> 54.6 us
  Pallas kernels: 51.2 us -> 137 us
  blocking collectives: 29.3 us -> 0 us
  other arithmetic: 7.29 us -> 0.76 us
    all_gather x3 -> x1, waiting for transfers between devices: 342 us -> 54.6 us  [body(): m = lax.all_gather(mine, 'row', axis=0)]
    pallas_call x0 -> x1, Pallas kernels: none -> 86.7 us  [gather(): pl.pallas_call(gather_kernel, out_shape=[jax.ShapeDtypeStruct((4, 64, 128...]
    reduce_scatter x1 -> x0, waiting for transfers between devices: 71.4 us -> none  [body(): lax.psum_scatter(term_block.reshape(per_owner * row_count, block_width),...]
    all_gather x1 -> x0, blocking collectives: 29.3 us -> none  [body(): mcols = lax.all_gather(grid_tile[0], 'row', axis=0, tiled=True).T]
  transfers between devices with their start and end apart: 4 -> 1, of which waited for: 4 -> 1; matrix products, arithmetic and copies ran while one was open for 0% -> 0% of each run, Pallas kernels for 0% -> 0%
where the time goes in v2:
time: 211 us; the launch traced here: 208 us
  Pallas kernels  137 us (65%)
  waiting for transfers between devices  54.6 us (26%)
  between operations  13.6 us (6%)
    pallas_call x1, Pallas kernels, gather(): pl.pallas_call(gather_kernel, out_shape=[jax.ShapeDtypeStruct((4, 64, 128...  86.7 us
    all_gather x1, waiting for transfers between devices, body(): m = lax.all_gather(mine, 'row', axis=0)  54.6 us
    pallas_call x1, Pallas kernels, finish(): pl.pallas_call(finish_kernel, out_shape=jax.ShapeDtypeStruct(tile.shape,...  50.7 us
  transfers between devices with their start and end apart: 1, of which 1 were waited for; matrix products, arithmetic and copies ran while one was open for 0% of the time, Pallas kernels for 0%

profile of v2, /device:TPU:1, one launch (start us, length us, event | category | flops | bytes accessed | tf_op | source)
XLA Modules:
  0.0 208.0 jit_solution(12997739044014697924)
XLA Ops:
  6.5 0.0 all-gather.3.cloned.1.call-start
  6.5 0.0 copy-start
  6.5 0.9 copy-done
  7.4 0.0 copy-start.1
  7.4 0.7 copy-done.1
  8.1 86.7 %gather.1 = (f32[4,64,128]{2,1,0:T(8,128)S(1)}, f32[8,4,64,128]{3,2,1,0:T(8,128)S(1)}) custom-call(bf16[128,512]{1,0:T(8,128)(2,1)S(1)} %copy-done, f32[1,128]{1,0:T(1,128)S(1)} %bitcast.4), custom_call_target="tpu_custom_call" | custom-call | tf_op jit(solution)/shard_map/gather/pallas_call | solution.py:156
  94.8 0.8 pad_maximum_fusion
  95.6 0.0 all-gather.3.cloned.1.call-update
  95.6 54.6 %all-gather.3.cloned.1.call-done = f32[144,64,128]{2,1,0:T(8,128)} async-done(((f32[9,64,128]{2,1,0:T(8,128)}), f32[144,64,128]{2,1,0:T(8,128)}) %all-gather.3.cloned.1.call-update) | async-done | bytes 4718608 | tf_op jit(solution)/shard_map/all_gather | solution.py:313
  150.2 50.7 %finish.1 = f32[4,64,128]{2,1,0:T(8,128)} custom-call(f32[16,9,64,128]{3,2,1,0:T(8,128)} %bitcast.5, f32[8,4,64,128]{3,2,1,0:T(8,128)S(1)} %get-tuple-element.7.band_ref, f32[4,64,128]{2,1,0:T(8,128)S(1)} %get-tuple-element.8.tile_ref), custom_call_target="tpu_custom_call" | custom-call | tf_op jit(solution)/shard_map/finish/pallas_call | solution.py:297
  (2 shorter events, 0.0 us)
Async XLA Ops:
  6.5 143.7 %all-gather.3.cloned.1.call-start = ((), (), s32[]{:S(2)}) async-start(), calls=%async_computation | async-start | bytes 5013504 | tf_op jit(solution)/shard_map/all_gather | solution.py:313
  6.5 0.9 copy-start
  7.4 0.7 copy-start.1
Sparse Core Ops, SparseCore 0:
  95.7 54.4 all-gather.2

commit v3 on v1

v3 whole, which is shorter than its diff:
```python
import jax
import jax.numpy as jnp
from jax import lax
from jax.experimental import pallas as pl
from jax.experimental.pallas import tpu as pltpu
from jax.sharding import PartitionSpec as P

PANEL = 1024
RING = 16
CHUNKS = 2
GROUPS = ((0, 2, 0), (2, 1, 0), (3, 2, 4), (5, 4, 8))
HI = lax.Precision.HIGHEST
MESH = pl.DeviceIdType.MESH


def bl(x, lane):
    return jnp.broadcast_to(x[:, lane:lane+1], (8, 128))
def bs(x, row):
    return jnp.broadcast_to(x[row:row+1, :], (8, 128))

def factor(S, E):
    sub = lax.broadcasted_iota(jnp.int32, (8, 128), 0)
    U, V = [], []
    n = len(S)
    S = list(S); E = list(E)
    for b in range(n):
        C = [bl(S[b], 8*b+i) for i in range(8)]
        s = {}
        for i in range(8):
            for t in range(i, 8):
                s[t, i] = bs(C[i], t)
        R = [bs(S[b], i) for i in range(8)]
        Q = [bs(E[b], i) for i in range(8)]
        rd, l = [], {}
        for i in range(8):
            rd.append(1.0 / s[i, i])
            for t in range(i+1, 8):
                l[t, i] = s[t, i] * rd[i]
            for u in range(i+1, 8):
                for t in range(u, 8):
                    s[t, u] = s[t, u] - l[t, i] * s[u, i]
            for t in range(i+1, 8):
                R[t] = R[t] - l[t, i] * R[i]
                Q[t] = Q[t] - l[t, i] * Q[i]
        ru = [lax.rsqrt(s[i, i]) for i in range(8)]
        Uo = R[0] * ru[0]; Vo = Q[0] * ru[0]
        for i in range(1, 8):
            Uo = jnp.where(sub == i, R[i] * ru[i], Uo)
            Vo = jnp.where(sub == i, Q[i] * ru[i], Vo)
        U.append(Uo); V.append(Vo)
        if b == n-1: break
        Z = [None]*8; Y = [None]*8
        for i in range(7, -1, -1):
            z = R[i] * rd[i]; y = Q[i] * rd[i]
            for t in range(7, i, -1):
                z = z - l[t, i] * Z[t]
                y = y - l[t, i] * Y[t]
            Z[i] = z; Y[i] = y
        for g in range(b+1, n):
            c = [bl(S[g], 8*b+i) for i in range(8)]
            a0 = c[0]*Z[0]; a1 = c[1]*Z[1]; e0 = c[0]*Y[0]; e1 = c[1]*Y[1]
            for i in range(2, 8, 2):
                a0 = a0 + c[i]*Z[i]; a1 = a1 + c[i+1]*Z[i+1]
                e0 = e0 + c[i]*Y[i]; e1 = e1 + c[i+1]*Y[i+1]
            S[g] = S[g] - (a0 + a1)
            E[g] = E[g] - (e0 + e1)
    return U, V


def dt(a, b):
    return lax.dot_general(a, b, (((1,), (1,)), ((), ())), precision=HI, preferred_element_type=jnp.float32)


def whole_kernel(x_ref, reg_ref, out_ref, tile_ref, m_ref, band_ref, L, B, T, xg, wc, wt, prod, parts, halves,
                 ring_send, ring_recv, pair_send, pair_recv, part_send, part_recv, hub_send, hub_recv,
                 near_send, near_recv, row_send, row_recv):
    r = lax.axis_index("row")
    c = lax.axis_index("col")
    h = c // RING
    z = c % RING
    q = z % 8
    other = 1 - h
    chip = r // 2
    core = r % 2
    partner = other * RING + z

    def along(distance):
        return h * RING + (z + distance + RING) % RING

    right, left = along(1), along(-1)
    hubs = (partner, along(8), other * RING + (z + 8) % RING)
    near = (1, -1, 2, -2, 3, -3, 4)

    barrier = pltpu.get_barrier_semaphore()
    for place in hubs + tuple(along(d) for d in near) + (along(-4),):
        pl.semaphore_signal(barrier, inc=1, device_id=(r, place), device_id_type=MESH)
    for step in range(1, 16):
        pl.semaphore_signal(barrier, inc=1, device_id=((r + step) % 16, c), device_id_type=MESH)
    pl.semaphore_wait(barrier, 26)

    def remote(src, dst, send, recv, device):
        return pltpu.make_async_remote_copy(
            src_ref=src, dst_ref=dst, send_sem=send, recv_sem=recv, device_id=device, device_id_type=MESH
        )

    swap = remote(x_ref, wc.at[h], pair_send.at[0], pair_recv.at[0], (r, partner))

    def ring_copy(way, step, chunk):
        owner = (z - step + 1 + RING) % RING if way == 0 else (z + step - 1) % RING
        rows = pl.ds(128 // CHUNKS * chunk, 128 // CHUNKS)
        src = x_ref.at[rows] if step == 1 else xg.at[owner, rows]
        return remote(src, xg.at[owner, rows], ring_send.at[way, step - 1, chunk],
                      ring_recv.at[way, step - 1, chunk], (r, right if way == 0 else left))

    steps = (8, 7)
    for chunk in range(CHUNKS):
        for way in range(2):
            ring_copy(way, 1, chunk).start()
    swap.start()
    wc[h] = x_ref[...]

    def multiply(owner, block):
        product = jnp.dot(block, wt[...], preferred_element_type=jnp.float32)
        prod[owner] = product.reshape(2, 64, 256)
        place = owner % 8
        half_k = owner // 8
        for to in range(2):
            mine = jnp.logical_and(place == chip, core == to)

            @pl.when(jnp.logical_not(mine))
            def _():
                remote(prod.at[owner, to], parts.at[half_k, r], part_send, part_recv.at[half_k],
                       (2 * place + to, c)).start()

            @pl.when(mine)
            def _():
                parts[half_k, r] = prod[owner, to]

    for step in range(1, 9):
        for chunk in range(CHUNKS):
            for way in range(2):
                if step <= steps[way]:
                    ring_copy(way, step, chunk).wait_recv()
                    if step < steps[way]:
                        ring_copy(way, step + 1, chunk).start()
        if step == 1:
            swap.wait()
            wt[...] = wc[...].reshape(256, 512).T
            multiply(z, x_ref[...])
        for way in range(2):
            if step <= steps[way]:
                owner = (z - step + RING) % RING if way == 0 else (z + step) % RING
                multiply(owner, xg[owner])

    lane = lax.broadcasted_iota(jnp.int32, (64, 128), 1)
    sub = lax.broadcasted_iota(jnp.int32, (64, 128), 0)
    for half_k in range(2):
        pltpu.make_async_copy(parts.at[half_k, pl.ds(0, 15)], parts.at[half_k, pl.ds(0, 15)], part_recv.at[half_k]).wait()
        total = parts[half_k, 0]
        for source in range(1, 16):
            total = total + parts[half_k, source]
        for side in range(2):
            block = total[:, 128 * side:128 * side + 128]
            hit = jnp.logical_and(chip + 8 * half_k == z, h == side)
            diagonal = jnp.logical_and(lane == sub + 64 * core, hit)
            halves[side, half_k] = block + jnp.where(diagonal, jnp.broadcast_to(reg_ref[...], (64, 128)), 0.0)

    give = remote(halves.at[other], tile_ref.at[pl.ds(2 * h, 2)], pair_send.at[1], pair_recv.at[1], (r, partner))
    lead = [remote(halves.at[0, 0], m_ref.at[r, 1 + q], hub_send.at[0, i], hub_recv.at[0], (r, hubs[i])) for i in range(3)]
    second = [remote(halves.at[0, 1], band_ref.at[q, 0], hub_send.at[1, i], hub_recv.at[1], (r, hubs[i])) for i in range(3)]
    third = [remote(halves.at[0], band_ref.at[q, pl.ds(1, 2)], hub_send.at[2, i], hub_recv.at[2], (r, hubs[i])) for i in range(3)]
    source0 = jnp.logical_and(z < 8, h == 0)
    source1 = jnp.logical_and(z < 8, h == 1)

    @pl.when(source0)
    def _():
        for copy in lead + second:
            copy.start()
        m_ref[r, 1 + q] = halves[0, 0]
        band_ref[q, 0] = halves[0, 1]

    @pl.when(source1)
    def _():
        for copy in third:
            copy.start()
        band_ref[q, pl.ds(1, 2)] = halves[0]

    give.start()
    tile_ref[pl.ds(2 * h, 2)] = halves[h]

    @pl.when(jnp.logical_not(source0))
    def _():
        lead[0].wait_recv()

    near_copies = [remote(m_ref.at[r, 1 + q], m_ref.at[r, 1 + q], near_send.at[0, i], near_recv.at[0, i], (r, along(d)))
                   for i, d in enumerate(near)]
    band_copies = [remote(band_ref.at[q], band_ref.at[q], near_send.at[1, i], near_recv.at[1, i], (r, along(d)))
                   for i, d in enumerate(near)]
    for copy in near_copies:
        copy.start()

    @pl.when(jnp.logical_not(source0))
    def _():
        second[0].wait_recv()

    @pl.when(jnp.logical_not(source1))
    def _():
        third[0].wait_recv()

    give.wait()
    m_ref[r, 0] = tile_ref[0]
    for copy in near_copies:
        copy.wait_recv()

    def row_copy(group, step):
        at, count, _ = GROUPS[group]
        part = m_ref.at[r, pl.ds(at, count)]
        return remote(part, part, row_send.at[group, step - 1], row_recv.at[group], ((r + step) % 16, c))

    def row_wait(group):
        at, count, low = GROUPS[group]

        def arrive(sources):
            part = m_ref.at[pl.ds(0, sources), pl.ds(at, count)]
            pltpu.make_async_copy(part, part, row_recv.at[group]).wait()

        if low == 0:
            arrive(15)
        else:
            pl.when(r >= low)(lambda: arrive(15 - low))
            pl.when(r < low)(lambda: arrive(16 - low))

    def row_sends(group, act):
        def each():
            for step in range(1, 16):
                act(row_copy(group, step))

        if GROUPS[group][2] == 0:
            each()
        else:
            pl.when(r >= GROUPS[group][2])(each)

    for group in range(len(GROUPS)):
        row_sends(group, lambda copy: copy.start())
        if group == 0:
            for copy in band_copies:
                copy.start()
    row_wait(0)

    lane = lax.broadcasted_iota(jnp.int32, (8, 128), 1)
    sub = lax.broadcasted_iota(jnp.int32, (8, 128), 0)
    E0 = [jnp.where(lane == sub + 8 * g, 1.0, 0.0).astype(jnp.float32) for g in range(16)]
    R = L.shape[0]

    def pieces(J):
        above = 2 * J
        yield 128 * J, 1024 - 128 * J, m_ref[above:, 1 + J].reshape(1024 - 128 * J, 128)
        yield 1024, 192, band_ref[J].reshape(192, 128)
        yield 1216, 128, m_ref[above:above + 2, 0].reshape(128, 128).T

    B[pl.ds(0, 1024), :] = m_ref[:, 1].reshape(1024, 128)
    B[pl.ds(1216, 128), :] = m_ref[:2, 0].reshape(128, 128).T
    for J in range(8):
        j0 = 128 * J
        r0 = j0 + 128
        r1 = r0 + 128
        S = [B[pl.ds(j0 + 8 * g, 8), :] for g in range(16)]
        U, V = factor(S, E0)
        if J == 0:
            for copy in band_copies:
                copy.wait_recv()
            B[pl.ds(1024, 192), :] = band_ref[0].reshape(192, 128)
        for group in range(1, len(GROUPS)):
            if GROUPS[group][0] == J + 2:
                row_wait(group)
        if J < 7:
            for at, count, value in pieces(J + 1):
                if J > 0:
                    value = value - dt(L[pl.ds(at, count), pl.ds(0, j0)], L[pl.ds(r0, 128), pl.ds(0, j0)])
                T[pl.ds(at, count), :] = value
        Um = jnp.concatenate([jnp.where(lane >= sub + 8 * g, U[g], 0.0) for g in range(16)], 0)
        Vm = jnp.concatenate(V, 0)
        L[pl.ds(j0, 128), pl.ds(j0, 128)] = Um.T
        if J < 7:
            Pn = dt(B[pl.ds(r0, 128), :], Vm)
            L[pl.ds(r0, 128), pl.ds(j0, 128)] = Pn
            Bn = T[pl.ds(r0, 128), :] - dt(Pn, Pn)
            Pr = dt(B[pl.ds(r1, R - r1), :], Vm)
            L[pl.ds(r1, R - r1), pl.ds(j0, 128)] = Pr
            B[pl.ds(r0, 128), :] = Bn
            B[pl.ds(r1, R - r1), :] = T[pl.ds(r1, R - r1), :] - dt(Pr, Pn)
        else:
            L[pl.ds(r0, R - r0), pl.ds(j0, 128)] = dt(B[pl.ds(r0, R - r0), :], Vm)
    for J in range(7):
        L[pl.ds(128 * J, 128), pl.ds(128 * (J + 1), 128 * (7 - J))] = jnp.zeros((128, 128 * (7 - J)), jnp.float32)
    tr = tile_ref[1:].reshape(192, 128) - dt(L[pl.ds(1024, 192), :], L[pl.ds(1216, 128), :])
    column = pl.multiple_of(jnp.minimum(c, 7) * 128, 128)
    first = L[pl.ds(pl.multiple_of(r * 64, 64), 64), pl.ds(column, 128)]
    solved = L[pl.ds(1024, 192), pl.ds(column, 128)]
    in_panel = c < 8
    out_ref[0] = jnp.where(in_panel, first, 0.0)
    out_ref[1:] = jnp.where(in_panel, solved, tr).reshape(3, 64, 128)

    for group in range(len(GROUPS)):
        row_sends(group, lambda copy: copy.wait_send())
    for way in range(2):
        for step in range(1, steps[way] + 1):
            for chunk in range(CHUNKS):
                ring_copy(way, step, chunk).wait_send()
    for copy in near_copies + band_copies:
        copy.wait_send()

    @pl.when(source0)
    def _():
        for copy in lead + second:
            copy.wait_send()

    @pl.when(source1)
    def _():
        for copy in third:
            copy.wait_send()

    pltpu.make_async_copy(prod.at[pl.ds(0, 15)], prod.at[pl.ds(0, 15)], part_send).wait()


def body(interactions, regular):
    vmem = pl.BlockSpec(memory_space=pltpu.VMEM)
    dma = pltpu.SemaphoreType.DMA
    rows = 1024 + 192 + 128
    return pl.pallas_call(
        whole_kernel,
        out_shape=jax.ShapeDtypeStruct((4, 64, 128), jnp.float32),
        in_specs=[vmem, vmem],
        out_specs=vmem,
        scratch_shapes=[
            pltpu.VMEM((4, 64, 128), jnp.float32),
            pltpu.VMEM((16, 9, 64, 128), jnp.float32),
            pltpu.VMEM((8, 3, 64, 128), jnp.float32),
            pltpu.VMEM((rows, PANEL), jnp.float32),
            pltpu.VMEM((rows, 128), jnp.float32),
            pltpu.VMEM((rows, 128), jnp.float32),
            pltpu.VMEM((RING, 128, 512), jnp.bfloat16),
            pltpu.VMEM((2, 128, 512), jnp.bfloat16),
            pltpu.VMEM((512, 256), jnp.bfloat16),
            pltpu.VMEM((RING, 2, 64, 256), jnp.float32),
            pltpu.VMEM((2, 16, 64, 256), jnp.float32),
            pltpu.VMEM((2, 2, 64, 128), jnp.float32),
            dma((2, 8, CHUNKS)),
            dma((2, 8, CHUNKS)),
            dma((2,)),
            dma((2,)),
            dma,
            dma((2,)),
            dma((3, 3)),
            dma((3,)),
            dma((2, 7)),
            dma((2, 7)),
            dma((len(GROUPS), 15)),
            dma((len(GROUPS),)),
        ],
        compiler_params=pltpu.CompilerParams(
            collective_id=0, has_side_effects=True, vmem_limit_bytes=50 * 1024 * 1024
        ),
        name="whole",
    )(interactions, regular.reshape(1, 128))


def solution(mesh):
    return jax.shard_map(
        body,
        mesh=mesh,
        in_specs=(P("col", "row"), P("col")),
        out_specs=P(None, "row", "col"),
        check_vma=False,
    )
```

time: 535 us -> 166 us (0.31)
  the two profiles are of different devices: /device:TPU:1 before, /device:TPU:57 now
where the time goes in v3:
time: 166 us; the launch traced here: 164 us
  Pallas kernels  161 us (97%)
  local copies, waits for them, and re-layouts  2.22 us (1%)
    pallas_call x1, Pallas kernels, body(): pl.pallas_call(whole_kernel, out_shape=jax.ShapeDtypeStruct((4, 64, 128),...  161 us

profile of v3, /device:TPU:57, one launch (start us, length us, event | category | flops | bytes accessed | tf_op | source)
XLA Modules:
  0.0 163.6 jit_solution(2466897515664886912)
XLA Ops:
  0.0 0.0 copy-start.1
  0.0 0.7 copy-done.1
  0.7 0.0 copy-start
  0.7 0.9 copy-done
  1.6 161.2 %whole.1 = f32[4,64,128]{2,1,0:T(8,128)S(1)} custom-call(bf16[128,512]{1,0:T(8,128)(2,1)S(1)} %copy-done, f32[1,128]{1,0:T(1,128)S(1)} %bitcast.1), custom_call_target="tpu_custom_call" | custom-call | tf_op jit(solution)/shard_map/whole/pallas_call | solution.py:330
  162.7 0.7 copy.4
Async XLA Ops:
  0.0 0.7 copy-start.1
  0.7 0.9 copy-start

commit v4 on v3

--- a/solution.py
+++ b/solution.py
@@ -8,7 +8,9 @@
 PANEL = 1024
 RING = 16
 CHUNKS = 2
-GROUPS = ((0, 2, 0), (2, 1, 0), (3, 2, 4), (5, 4, 8))
+GROUPS = ((0, 1, 1), (1, 1, 1), (2, 2, 2), (4, 4, 4), (8, 1, 0))
+OWN = 4
+FURTHER = ((), (), (), (0, 1), (2, 3), (4,), (5,), (6,))
 HI = lax.Precision.HIGHEST
 MESH = pl.DeviceIdType.MESH
 
@@ -18,19 +20,25 @@
 def bs(x, row):
     return jnp.broadcast_to(x[row:row+1, :], (8, 128))
 
-def factor(S, E):
+def factor(S, E, scr, middle):
     sub = lax.broadcasted_iota(jnp.int32, (8, 128), 0)
     U, V = [], []
     n = len(S)
     S = list(S); E = list(E)
     for b in range(n):
+        if b == n // 2:
+            middle()
         C = [bl(S[b], 8*b+i) for i in range(8)]
         s = {}
         for i in range(8):
+            scr[b, i] = C[i]
+        for i in range(8):
             for t in range(i, 8):
-                s[t, i] = bs(C[i], t)
-        R = [bs(S[b], i) for i in range(8)]
-        Q = [bs(E[b], i) for i in range(8)]
+                s[t, i] = jnp.broadcast_to(scr[b, i, pl.ds(t, 1), :], (8, 128))
+        scr[b, 8] = S[b]
+        scr[b, 9] = E[b]
+        R = [jnp.broadcast_to(scr[b, 8, pl.ds(i, 1), :], (8, 128)) for i in range(8)]
+        Q = [jnp.broadcast_to(scr[b, 9, pl.ds(i, 1), :], (8, 128)) for i in range(8)]
         rd, l = [], {}
         for i in range(8):
             rd.append(1.0 / s[i, i])
@@ -71,9 +79,9 @@
     return lax.dot_general(a, b, (((1,), (1,)), ((), ())), precision=HI, preferred_element_type=jnp.float32)
 
 
-def whole_kernel(x_ref, reg_ref, out_ref, tile_ref, m_ref, band_ref, L, B, T, xg, wc, wt, prod, parts, halves,
+def whole_kernel(x_ref, reg_ref, out_ref, tile_ref, m_ref, band_ref, L, B, T, Vs, scr, xg, wc, wt, prod, parts, halves,
                  ring_send, ring_recv, pair_send, pair_recv, part_send, part_recv, hub_send, hub_recv,
-                 near_send, near_recv, row_send, row_recv):
+                 near_send, near_recv, top_send, top_recv, row_send, row_recv, core_send, core_recv):
     r = lax.axis_index("row")
     c = lax.axis_index("col")
     h = c // RING
@@ -82,6 +90,7 @@
     other = 1 - h
     chip = r // 2
     core = r % 2
+    sibling = 2 * chip + 1 - core
     partner = other * RING + z
 
     def along(distance):
@@ -89,7 +98,7 @@
 
     right, left = along(1), along(-1)
     hubs = (partner, along(8), other * RING + (z + 8) % RING)
-    near = (1, -1, 2, -2, 3, -3, 4)
+    near = (1, 2, 3, 4, -3, -2, -1)
 
     barrier = pltpu.get_barrier_semaphore()
     for place in hubs + tuple(along(d) for d in near) + (along(-4),):
@@ -166,7 +175,7 @@
             halves[side, half_k] = block + jnp.where(diagonal, jnp.broadcast_to(reg_ref[...], (64, 128)), 0.0)
 
     give = remote(halves.at[other], tile_ref.at[pl.ds(2 * h, 2)], pair_send.at[1], pair_recv.at[1], (r, partner))
-    lead = [remote(halves.at[0, 0], m_ref.at[r, 1 + q], hub_send.at[0, i], hub_recv.at[0], (r, hubs[i])) for i in range(3)]
+    lead = [remote(halves.at[0, 0], m_ref.at[chip, core, q], hub_send.at[0, i], hub_recv.at[0], (r, hubs[i])) for i in range(3)]
     second = [remote(halves.at[0, 1], band_ref.at[q, 0], hub_send.at[1, i], hub_recv.at[1], (r, hubs[i])) for i in range(3)]
     third = [remote(halves.at[0], band_ref.at[q, pl.ds(1, 2)], hub_send.at[2, i], hub_recv.at[2], (r, hubs[i])) for i in range(3)]
     source0 = jnp.logical_and(z < 8, h == 0)
@@ -174,9 +183,16 @@
 
     @pl.when(source0)
     def _():
-        for copy in lead + second:
+        for copy in lead:
             copy.start()
-        m_ref[r, 1 + q] = halves[0, 0]
+        m_ref[chip, core, q] = halves[0, 0]
+
+    give.start()
+
+    @pl.when(source0)
+    def _():
+        for copy in second:
+            copy.start()
         band_ref[q, 0] = halves[0, 1]
 
     @pl.when(source1)
@@ -185,124 +201,179 @@
             copy.start()
         band_ref[q, pl.ds(1, 2)] = halves[0]
 
-    give.start()
     tile_ref[pl.ds(2 * h, 2)] = halves[h]
-
-    @pl.when(jnp.logical_not(source0))
-    def _():
-        lead[0].wait_recv()
-
-    near_copies = [remote(m_ref.at[r, 1 + q], m_ref.at[r, 1 + q], near_send.at[0, i], near_recv.at[0, i], (r, along(d)))
-                   for i, d in enumerate(near)]
-    band_copies = [remote(band_ref.at[q], band_ref.at[q], near_send.at[1, i], near_recv.at[1, i], (r, along(d)))
-                   for i, d in enumerate(near)]
-    for copy in near_copies:
-        copy.start()
-
-    @pl.when(jnp.logical_not(source0))
-    def _():
-        second[0].wait_recv()
-
-    @pl.when(jnp.logical_not(source1))
-    def _():
-        third[0].wait_recv()
-
-    give.wait()
-    m_ref[r, 0] = tile_ref[0]
-    for copy in near_copies:
-        copy.wait_recv()
 
     def row_copy(group, step):
         at, count, _ = GROUPS[group]
-        part = m_ref.at[r, pl.ds(at, count)]
-        return remote(part, part, row_send.at[group, step - 1], row_recv.at[group], ((r + step) % 16, c))
-
-    def row_wait(group):
-        at, count, low = GROUPS[group]
-
-        def arrive(sources):
-            part = m_ref.at[pl.ds(0, sources), pl.ds(at, count)]
-            pltpu.make_async_copy(part, part, row_recv.at[group]).wait()
-
-        if low == 0:
-            arrive(15)
-        else:
-            pl.when(r >= low)(lambda: arrive(15 - low))
-            pl.when(r < low)(lambda: arrive(16 - low))
+        part = m_ref.at[chip, core, pl.ds(at, count)]
+        return remote(part, part, row_send.at[group, step - 1], row_recv.at[group], ((r + 2 * step) % 16, c))
 
     def row_sends(group, act):
         def each():
-            for step in range(1, 16):
+            for step in range(1, 8):
                 act(row_copy(group, step))
 
         if GROUPS[group][2] == 0:
             each()
         else:
-            pl.when(r >= GROUPS[group][2])(each)
-
-    for group in range(len(GROUPS)):
-        row_sends(group, lambda copy: copy.start())
-        if group == 0:
-            for copy in band_copies:
-                copy.start()
-    row_wait(0)
+            pl.when(chip >= GROUPS[group][2])(each)
+
+    def core_copy(group):
+        at, count, low = GROUPS[group]
+        part = m_ref.at[pl.ds(low, 8 - low), core, pl.ds(at, count)]
+        return remote(part, part, core_send.at[group], core_recv.at[group], (sibling, c))
+
+    def row_pass(group):
+        at, count, low = GROUPS[group]
+
+        def arrive(sources):
+            part = m_ref.at[pl.ds(0, sources), 0, pl.ds(at, count)]
+            pltpu.make_async_copy(part, part, row_recv.at[group]).wait()
+
+        if low == 0:
+            arrive(7)
+        else:
+            pl.when(chip >= low)(lambda: arrive(7 - low))
+            pl.when(chip < low)(lambda: arrive(8 - low))
+        core_copy(group).start()
+
+    def top_copy(band, step):
+        part = m_ref.at[0, band, 0]
+        return remote(part, part, top_send.at[step - 1], top_recv.at[band], ((r + step) % 16, c))
+
+    def top_sends(act):
+        for band in range(2):
+            @pl.when(r == band)
+            def _():
+                for step in range(1, 16):
+                    act(top_copy(band, step))
+
+    @pl.when(jnp.logical_not(source0))
+    def _():
+        lead[0].wait_recv()
+
+    mine = m_ref.at[chip, core, q]
+    near_copies = [remote(mine, mine, near_send.at[0, i], near_recv.at[0, i], (r, along(d))) for i, d in enumerate(near)]
+    band_copies = [remote(band_ref.at[q], band_ref.at[q], near_send.at[1, i], near_recv.at[1, i], (r, along(d)))
+                   for i, d in enumerate(near)]
+
+    @pl.when(q < 2)
+    def _():
+        for copy in near_copies:
+            copy.start()
+
+    give.wait()
+    m_ref[chip, core, 8] = tile_ref[0]
+    row_sends(OWN, lambda copy: copy.start())
+    for i in range(7):
+        pl.when(q == i + 1)(near_copies[i].wait_recv)
+    top_sends(lambda copy: copy.start())
+    row_sends(0, lambda copy: copy.start())
+    for i in range(7):
+        pl.when(q == (i + 2) % 8)(near_copies[i].wait_recv)
+    row_sends(1, lambda copy: copy.start())
+
+    @pl.when(q >= 2)
+    def _():
+        for copy in near_copies:
+            copy.start()
+
+    @pl.when(jnp.logical_not(source0))
+    def _():
+        second[0].wait_recv()
+
+    @pl.when(jnp.logical_not(source1))
+    def _():
+        third[0].wait_recv()
+
+    for copy in band_copies:
+        copy.start()
+
+    for band in range(2):
+        @pl.when(r != band)
+        def _():
+            top_copy(band, 1).wait_recv()
 
     lane = lax.broadcasted_iota(jnp.int32, (8, 128), 1)
     sub = lax.broadcasted_iota(jnp.int32, (8, 128), 0)
     E0 = [jnp.where(lane == sub + 8 * g, 1.0, 0.0).astype(jnp.float32) for g in range(16)]
-    R = L.shape[0]
-
-    def pieces(J):
-        above = 2 * J
-        yield 128 * J, 1024 - 128 * J, m_ref[above:, 1 + J].reshape(1024 - 128 * J, 128)
-        yield 1024, 192, band_ref[J].reshape(192, 128)
-        yield 1216, 128, m_ref[above:above + 2, 0].reshape(128, 128).T
-
-    B[pl.ds(0, 1024), :] = m_ref[:, 1].reshape(1024, 128)
-    B[pl.ds(1216, 128), :] = m_ref[:2, 0].reshape(128, 128).T
+
+    def further(K):
+        k0 = 128 * K
+        value = jnp.concatenate([band_ref[K].reshape(192, 128), m_ref[K, :, 8].reshape(128, 128).T], 0)
+        if K > 0:
+            value = value - dt(L[pl.ds(1024, 320), pl.ds(0, k0)], L[pl.ds(k0, 128), pl.ds(0, k0)])
+        L[pl.ds(1024, 320), pl.ds(k0, 128)] = dt(value, Vs[K])
+
+    def middle(J):
+        if J == 0:
+            row_pass(0)
+            row_pass(OWN)
+        elif J == 1:
+            row_pass(2)
+        elif J == 2:
+            row_pass(3)
+
+    def after(J):
+        if J == 0:
+            row_pass(1)
+            for i in range(7):
+                pl.when(jnp.logical_and(q != i + 1, q != (i + 2) % 8))(near_copies[i].wait_recv)
+            row_sends(2, lambda copy: copy.start())
+            row_sends(3, lambda copy: copy.start())
+            core_copy(0).wait_recv()
+            B[pl.ds(128, 896), :] = m_ref[1:, :, 0].reshape(896, 128)
+            core_copy(1).wait_recv()
+        elif J == 1:
+            core_copy(2).wait_recv()
+        elif J == 3:
+            core_copy(3).wait_recv()
+            core_copy(OWN).wait_recv()
+            for copy in band_copies:
+                copy.wait_recv()
+
+    B[pl.ds(0, 128), :] = m_ref[0, :, 0].reshape(128, 128)
     for J in range(8):
         j0 = 128 * J
         r0 = j0 + 128
         r1 = r0 + 128
         S = [B[pl.ds(j0 + 8 * g, 8), :] for g in range(16)]
-        U, V = factor(S, E0)
-        if J == 0:
-            for copy in band_copies:
-                copy.wait_recv()
-            B[pl.ds(1024, 192), :] = band_ref[0].reshape(192, 128)
-        for group in range(1, len(GROUPS)):
-            if GROUPS[group][0] == J + 2:
-                row_wait(group)
+        U, V = factor(S, E0, scr, lambda: middle(J))
+        after(J)
         if J < 7:
-            for at, count, value in pieces(J + 1):
-                if J > 0:
-                    value = value - dt(L[pl.ds(at, count), pl.ds(0, j0)], L[pl.ds(r0, 128), pl.ds(0, j0)])
-                T[pl.ds(at, count), :] = value
+            value = m_ref[J + 1:, :, J + 1].reshape(1024 - r0, 128)
+            if J > 0:
+                value = value - dt(L[pl.ds(r0, 1024 - r0), pl.ds(0, j0)], L[pl.ds(r0, 128), pl.ds(0, j0)])
+            T[pl.ds(r0, 1024 - r0), :] = value
+        for K in FURTHER[J]:
+            further(K)
         Um = jnp.concatenate([jnp.where(lane >= sub + 8 * g, U[g], 0.0) for g in range(16)], 0)
         Vm = jnp.concatenate(V, 0)
+        Vs[J] = Vm
         L[pl.ds(j0, 128), pl.ds(j0, 128)] = Um.T
         if J < 7:
             Pn = dt(B[pl.ds(r0, 128), :], Vm)
             L[pl.ds(r0, 128), pl.ds(j0, 128)] = Pn
-            Bn = T[pl.ds(r0, 128), :] - dt(Pn, Pn)
-            Pr = dt(B[pl.ds(r1, R - r1), :], Vm)
-            L[pl.ds(r1, R - r1), pl.ds(j0, 128)] = Pr
-            B[pl.ds(r0, 128), :] = Bn
-            B[pl.ds(r1, R - r1), :] = T[pl.ds(r1, R - r1), :] - dt(Pr, Pn)
-        else:
-            L[pl.ds(r0, R - r0), pl.ds(j0, 128)] = dt(B[pl.ds(r0, R - r0), :], Vm)
+            B[pl.ds(r0, 128), :] = T[pl.ds(r0, 128), :] - dt(Pn, Pn)
+        if J < 6:
+            Pr = dt(B[pl.ds(r1, 1024 - r1), :], Vm)
+            L[pl.ds(r1, 1024 - r1), pl.ds(j0, 128)] = Pr
+            B[pl.ds(r1, 1024 - r1), :] = T[pl.ds(r1, 1024 - r1), :] - dt(Pr, Pn)
+    further(7)
     for J in range(7):
         L[pl.ds(128 * J, 128), pl.ds(128 * (J + 1), 128 * (7 - J))] = jnp.zeros((128, 128 * (7 - J)), jnp.float32)
     tr = tile_ref[1:].reshape(192, 128) - dt(L[pl.ds(1024, 192), :], L[pl.ds(1216, 128), :])
     column = pl.multiple_of(jnp.minimum(c, 7) * 128, 128)
-    first = L[pl.ds(pl.multiple_of(r * 64, 64), 64), pl.ds(column, 128)]
+    top = L[pl.ds(pl.multiple_of(r * 64, 64), 64), pl.ds(column, 128)]
     solved = L[pl.ds(1024, 192), pl.ds(column, 128)]
     in_panel = c < 8
-    out_ref[0] = jnp.where(in_panel, first, 0.0)
+    out_ref[0] = jnp.where(in_panel, top, 0.0)
     out_ref[1:] = jnp.where(in_panel, solved, tr).reshape(3, 64, 128)
 
+    top_sends(lambda copy: copy.wait_send())
     for group in range(len(GROUPS)):
         row_sends(group, lambda copy: copy.wait_send())
+        core_copy(group).wait_send()
     for way in range(2):
         for step in range(1, steps[way] + 1):
             for chunk in range(CHUNKS):
@@ -334,11 +405,13 @@
         out_specs=vmem,
         scratch_shapes=[
             pltpu.VMEM((4, 64, 128), jnp.float32),
-            pltpu.VMEM((16, 9, 64, 128), jnp.float32),
+            pltpu.VMEM((8, 2, 9, 64, 128), jnp.float32),
             pltpu.VMEM((8, 3, 64, 128), jnp.float32),
             pltpu.VMEM((rows, PANEL), jnp.float32),
             pltpu.VMEM((rows, 128), jnp.float32),
             pltpu.VMEM((rows, 128), jnp.float32),
+            pltpu.VMEM((8, 128, 128), jnp.float32),
+            pltpu.VMEM((16, 10, 8, 128), jnp.float32),
             pltpu.VMEM((RING, 128, 512), jnp.bfloat16),
             pltpu.VMEM((2, 128, 512), jnp.bfloat16),
             pltpu.VMEM((512, 256), jnp.bfloat16),
@@ -355,7 +428,11 @@
             dma((3,)),
             dma((2, 7)),
             dma((2, 7)),
-            dma((len(GROUPS), 15)),
+            dma((15,)),
+            dma((2,)),
+            dma((len(GROUPS), 7)),
+            dma((len(GROUPS),)),
+            dma((len(GROUPS),)),
             dma((len(GROUPS),)),
         ],
         compiler_params=pltpu.CompilerParams(

time: 166 us -> 142 us (0.86)
  the two profiles are of different devices: /device:TPU:57 before, /device:TPU:40 now
where the time goes in v4:
time: 142 us; the launch traced here: 140 us
  Pallas kernels  137 us (96%)
  local copies, waits for them, and re-layouts  2.22 us (2%)
    pallas_call x1, Pallas kernels, body(): pl.pallas_call(whole_kernel, out_shape=jax.ShapeDtypeStruct((4, 64, 128),...  137 us

profile of v4, /device:TPU:40, one launch (start us, length us, event | category | flops | bytes accessed | tf_op | source)
XLA Modules:
  0.0 139.6 jit_solution(17993453481808805668)
XLA Ops:
  0.0 0.0 copy-start.1
  0.0 0.7 copy-done.1
  0.7 0.0 copy-start
  0.7 0.9 copy-done
  1.6 137.2 %whole.1 = f32[4,64,128]{2,1,0:T(8,128)S(1)} custom-call(bf16[128,512]{1,0:T(8,128)(2,1)S(1)} %copy-done, f32[1,128]{1,0:T(1,128)S(1)} %bitcast.1), custom_call_target="tpu_custom_call" | custom-call | tf_op jit(solution)/shard_map/whole/pallas_call | solution.py:401
  138.8 0.7 copy.4
Async XLA Ops:
  0.0 0.7 copy-start.1
  0.7 0.9 copy-start
